TPU v7x, 32 devices: a whole 2x2x4 slice. The times are simulated.
32 devices in a mesh: groups: 2 (over x), expert: 16 (over z, y, core).
Axes of the slice: x: 2, y: 2, z: 4, core: 2. Of those that a mesh axis runs over, the one named last changes fastest.
Arguments:
- activations: bfloat16 [16, 256, 1536], P('expert', 'groups'), parts along dimension 1, may hold values from -6 to 6
- routing: int32 [256, 6], P('groups'), parts along dimension 0, may hold values from 0 to 15, all different within a row
- pairs: int32 [16, 3], replicated, may hold values from -1 to 15, as said below
Outputs:
- energy: float32 [16, 6, 1536], P('expert', 'groups'), parts along dimension 1
There are 2 independent parts, one for each index of `groups`. A program takes and returns all parts, laid end to end along the dimension named above; an argument that names none is the same for every part. Nothing has to cross between parts.
Inputs may be any that keep to these rules, and one draw needn't show every extreme that they name: `pairs`: experts fall into merge clusters of 8; each expert lists 1 to 3 distinct partners of its own cluster other than itself, used slots first and -1 after them; some expert uses all 3 slots and some only one.
All inputs are finite; a program needn't handle non-finite values.
Results may differ from a plain program's by a relative error of at most 0.0023.
Values may be sent and summed in bfloat16 or wider, within the bound.
A program may use at most 64 MiB of HBM per device.

v0:
```python
import jax
import jax.numpy as jnp
from jax import lax
from jax.sharding import PartitionSpec as P


def weights_for(routing, experts):
    labels = jnp.arange(experts, dtype=jnp.int32)
    hit = jnp.any(routing[:, :, None] == labels[None, None, :], axis=1)
    return 0.5 + 1.5 * hit.astype(jnp.float32)


def normed(values, weights, total):
    values = values.astype(jnp.float32)
    center = jnp.sum(weights[:, None] * values, axis=0) / total
    shifted = values - center[None, :]
    spread = jnp.sum(weights[:, None] * shifted * shifted, axis=0) / total
    scale = jnp.sqrt(weights / total)[:, None]
    return (shifted * scale / jnp.sqrt(spread[None, :] + 1e-06)).astype(jnp.bfloat16)


def energies(own, own_w, blocks, partner_w):
    count = blocks.shape[0]
    tokens = own.shape[0]
    width = own.shape[1]
    other = blocks.reshape(count, tokens, width)
    part_w = partner_w.reshape(count, tokens)

    def one_slot(items):
        weights = own_w * items[1].astype(jnp.float32)
        total = jnp.sum(weights)
        total = jnp.where(total > 0, total, 1.0)
        left = normed(own, weights, total)
        right = normed(items[0], weights, total)
        corr = jnp.dot(left.T, right, preferred_element_type=jnp.float32)
        return jnp.sum(corr * corr, axis=1)

    return lax.map(one_slot, (other, part_w))


def per_device(activations, routing, pairs):
    own = activations[0]
    experts = lax.axis_size("expert")
    me = lax.axis_index("expert")
    tokens = own.shape[0]
    width = own.shape[1]
    piece = tokens // experts
    columns = lax.all_to_all(
        own.reshape(experts, piece, width), "expert", split_axis=0, concat_axis=0, tiled=True
    )
    local_rows = lax.dynamic_slice_in_dim(routing, me * piece, piece, 0)
    local_table = weights_for(local_rows, experts)
    valid = (pairs >= 0).astype(jnp.float32)
    safe = jnp.maximum(pairs, 0).T
    send_blocks = columns[safe]
    send_weights = (local_table.T[safe] * valid.T[:, :, None]).astype(jnp.bfloat16)
    own_w = 0.5 + 1.5 * jnp.any(routing == me, axis=1).astype(jnp.float32)
    result = energies(
        own,
        own_w,
        lax.all_to_all(send_blocks, "expert", split_axis=1, concat_axis=1, tiled=True),
        lax.all_to_all(send_weights, "expert", split_axis=1, concat_axis=1, tiled=True),
    )
    return result[None]


def solution(mesh):
    return jax.shard_map(
        per_device,
        mesh=mesh,
        in_specs=(P("expert", "groups", None), P("groups", None), P()),
        out_specs=P("expert", "groups", None),
        check_vma=False,
    )
```

profile of v0, /device:TPU:13, one launch (start us, length us, event | category | flops | bytes accessed | tf_op | source)
XLA Modules:
  0.0 74.1 jit_solution(8252047136466737706)
XLA Ops:
  0.0 6.6 %all-to-all-start.1 = ((bf16[16,8,1536]{2,1,0:T(8,128)(2,1)}), bf16[16,8,1536]{2,1,0:T(8,128)(2,1)S(1)}, u32[]{:S(2)}, u32[]{:S(2)}) async-start(bf16[16,8,1536]{2,1,0:T(8,128)(2,1)} %bitcast.29), calls=%async_computation.1 | async-start | bytes 786432 | tf_op jit(solution)/shard_map/all_to_all | solution.py:48
  6.6 0.8 %constant_dynamic-slice_fusion = s32[8,6]{0,1:T(8,128)S(1)} fusion(s32[128,6]{0,1:T(8,128)} %param.6, s32[]{:T(128)S(6)} %select_n.11), kind=kLoop, calls=%fused_computation.44 | loop fusion | bytes 388 | tf_op jit(solution)/shard_map/dynamic_slice | solution.py:51
  7.3 0.1 fusion.21
  7.4 0.1 copy.27
  7.5 0.7 compare_select_fusion
  8.2 0.1 reshape.53
  8.3 0.6 gather_fusion
  8.9 0.1 copy.29
  8.9 0.7 convert_bitcast_fusion
  9.6 0.7 copy.30
  10.3 7.0 %all-to-all-done.1 = bf16[16,8,1536]{2,1,0:T(8,128)(2,1)S(1)} async-done(((bf16[16,8,1536]{2,1,0:T(8,128)(2,1)}), bf16[16,8,1536]{2,1,0:T(8,128)(2,1)S(1)}, u32[]{:S(2)}, u32[]{:S(2)}) %all-to-all-start.1) | async-done | bytes 393248 | tf_op jit(solution)/shard_map/all_to_all | solution.py:48
  17.3 5.0 %all-to-all-start = ((bf16[3,16,8]{2,0,1:T(4,128)(2,1)}), bf16[3,16,8]{2,0,1:T(4,128)(2,1)S(1)}, u32[]{:S(2)}, u32[]{:S(2)}) async-start(bf16[3,16,8]{2,0,1:T(4,128)(2,1)} %copy.30), calls=%async_computation | async-start | bytes 32768 | tf_op jit(solution)/shard_map/all_to_all | solution.py:62
  22.3 0.6 gather_fusion.1
  22.9 1.1 %copy.32 = bf16[3,16,8,1536]{3,2,0,1:T(8,128)(2,1)} copy(bf16[3,16,8,1536]{3,2,1,0:T(8,128)(2,1)S(1)} %bitcast.32) | data formatting | bytes 2359296 | tf_op jit(solution)/shard_map/gather | solution.py:55
  24.0 0.0 copy-start.1
  24.0 2.4 %all-to-all-done = bf16[3,16,8]{2,0,1:T(4,128)(2,1)S(1)} async-done(((bf16[3,16,8]{2,0,1:T(4,128)(2,1)}), bf16[3,16,8]{2,0,1:T(4,128)(2,1)S(1)}, u32[]{:S(2)}, u32[]{:S(2)}) %all-to-all-start) | async-done | bytes 800 | tf_op jit(solution)/shard_map/all_to_all | solution.py:62
  26.4 6.0 %all-to-all-start.2 = ((bf16[3,16,8,1536]{3,2,0,1:T(8,128)(2,1)}), bf16[3,16,8,1536]{3,2,0,1:T(8,128)(2,1)S(1)}, u32[]{:S(2)}, u32[]{:S(2)}) async-start(bf16[3,16,8,1536]{3,2,0,1:T(8,128)(2,1)} %copy.32), calls=%async_computation.2 | async-start | bytes 2359296 | tf_op jit(solution)/shard_map/all_to_all | solution.py:61
  32.4 0.0 copy-done.1
  32.5 0.1 reshape.47
  32.6 0.0 copy-start
  32.6 27.6 %all-to-all-done.2 = bf16[3,16,8,1536]{3,2,0,1:T(8,128)(2,1)S(1)} async-done(((bf16[3,16,8,1536]{3,2,0,1:T(8,128)(2,1)}), bf16[3,16,8,1536]{3,2,0,1:T(8,128)(2,1)S(1)}, u32[]{:S(2)}, u32[]{:S(2)}) %all-to-all-start.2) | async-done | bytes 1179680 | tf_op jit(solution)/shard_map/all_to_all | solution.py:61
  60.2 0.1 copy.37
  60.3 0.0 copy-done
  60.3 13.2 %while.10 = (s32[]{:T(128)}, f32[3,1536]{1,0:T(4,128)S(1)}, bf16[128,1536]{1,0:T(8,128)(2,1)S(1)}, bf16[3,128]{1,0:T(4,128)(2,1)S(1)}, f32[128]{0:T(128)S(1)}, /...) while((s32[]{:T(128)}, f32[3,1536]{1,0:T(4,128)S(1)}, ...), condition=%wide.region_9.10_spmd, body=%wide.region_2.9_spmd.sunk | while | flops 613812224 | bytes 2513827 | solution.py:38
  60.3 0.7 fusion.32
  62.4 0.2 fusion.33
  62.5 0.3 fusion.34
  62.8 0.2 fusion.35
  63.0 1.5 %fusion.36 = f32[1536]{0:T(1024)S(1)} fusion(bf16[128,1536]{1,0:T(8,128)(2,1)S(1)} %get-tuple-element.127, f32[1536]{0:T(1024)S(1)} %get-tuple-element.103, f32[1536]{0:T(1024)S(1)} %broadcast_divide_fusion.5, f32[1536]{0:T(1024)S(1)} %get-tuple-element.104, f32[128]{0:T(128)S(1)} %divide_sqrt_fusion.2, f32[1536]{0:T(1024)S(1)} %broadcast_divide_fusion.4, ...), kind=kOutput, calls=%fused_computation.3.clone.1 | convolution fusion | flops 610662912 | bytes 826372 | tf_op jit(solution)/shard_map/while/body/eval_jaxpr/dot_general | solution.py:35
  64.6 0.1 dynamic_update_slice.5
  64.7 0.7 fusion.32
  66.8 0.2 fusion.33
  67.0 0.3 fusion.34
  67.2 0.2 fusion.35
  67.4 1.5 %fusion.36 = f32[1536]{0:T(1024)S(1)} fusion(bf16[128,1536]{1,0:T(8,128)(2,1)S(1)} %get-tuple-element.127, f32[1536]{0:T(1024)S(1)} %get-tuple-element.103, f32[1536]{0:T(1024)S(1)} %broadcast_divide_fusion.5, f32[1536]{0:T(1024)S(1)} %get-tuple-element.104, f32[128]{0:T(128)S(1)} %divide_sqrt_fusion.2, f32[1536]{0:T(1024)S(1)} %broadcast_divide_fusion.4, ...), kind=kOutput, calls=%fused_computation.3.clone.1 | convolution fusion | flops 610662912 | bytes 826372 | tf_op jit(solution)/shard_map/while/body/eval_jaxpr/dot_general | solution.py:35
  69.0 0.1 dynamic_update_slice.5
  69.1 0.7 fusion.32
  71.2 0.2 fusion.33
  71.4 0.3 fusion.34
  71.7 0.2 fusion.35
  71.9 1.5 %fusion.36 = f32[1536]{0:T(1024)S(1)} fusion(bf16[128,1536]{1,0:T(8,128)(2,1)S(1)} %get-tuple-element.127, f32[1536]{0:T(1024)S(1)} %get-tuple-element.103, f32[1536]{0:T(1024)S(1)} %broadcast_divide_fusion.5, f32[1536]{0:T(1024)S(1)} %get-tuple-element.104, f32[128]{0:T(128)S(1)} %divide_sqrt_fusion.2, f32[1536]{0:T(1024)S(1)} %broadcast_divide_fusion.4, ...), kind=kOutput, calls=%fused_computation.3.clone.1 | convolution fusion | flops 610662912 | bytes 826372 | tf_op jit(solution)/shard_map/while/body/eval_jaxpr/dot_general | solution.py:35
  73.4 0.1 dynamic_update_slice.5
  73.5 0.6 broadcast_in_dim.11
  (22 shorter events, 0.2 us)
Async XLA Ops:
  0.0 17.3 %all-to-all-start.1 = ((bf16[16,8,1536]{2,1,0:T(8,128)(2,1)}), bf16[16,8,1536]{2,1,0:T(8,128)(2,1)S(1)}, u32[]{:S(2)}, u32[]{:S(2)}) async-start(bf16[16,8,1536]{2,1,0:T(8,128)(2,1)} %bitcast.29), calls=%async_computation.1 | async-start | bytes 786432 | tf_op jit(solution)/shard_map/all_to_all | solution.py:48
  17.3 9.1 %all-to-all-start = ((bf16[3,16,8]{2,0,1:T(4,128)(2,1)}), bf16[3,16,8]{2,0,1:T(4,128)(2,1)S(1)}, u32[]{:S(2)}, u32[]{:S(2)}) async-start(bf16[3,16,8]{2,0,1:T(4,128)(2,1)} %copy.30), calls=%async_computation | async-start | bytes 32768 | tf_op jit(solution)/shard_map/all_to_all | solution.py:62
  24.0 8.4 %copy-start.1 = (s32[128,6]{0,1:T(8,128)S(1)}, s32[128,6]{0,1:T(8,128)}, u32[]{:S(2)}) copy-start(s32[128,6]{0,1:T(8,128)} %param.6) | copy-start | bytes 9220
  26.4 33.8 %all-to-all-start.2 = ((bf16[3,16,8,1536]{3,2,0,1:T(8,128)(2,1)}), bf16[3,16,8,1536]{3,2,0,1:T(8,128)(2,1)S(1)}, u32[]{:S(2)}, u32[]{:S(2)}) async-start(bf16[3,16,8,1536]{3,2,0,1:T(8,128)(2,1)} %copy.32), calls=%async_computation.2 | async-start | bytes 2359296 | tf_op jit(solution)/shard_map/all_to_all | solution.py:61
  32.6 27.7 %copy-start = (bf16[1,128,1536]{2,1,0:T(8,128)(2,1)S(1)}, bf16[1,128,1536]{2,1,0:T(8,128)(2,1)}, u32[]{:S(2)}) copy-start(bf16[1,128,1536]{2,1,0:T(8,128)(2,1)} %param.5) | copy-start | bytes 1179652
where the time goes:
time: 74.6 us; the launch traced here: 74.1 us
  waiting for transfers between devices  37 us (50%)
  starting transfers between devices  17.5 us (23%)
  other arithmetic  5.44 us (7%)
  local copies, waits for them, and re-layouts  5.17 us (7%)
  matrix products  4.58 us (6%)
  loops' own time  4.39 us (6%)
    all_to_all x1, waiting for transfers between devices, per_device(): lax.all_to_all(send_blocks, 'expert', split_axis=1, concat_axis=1, tiled=...  27.6 us
    all_to_all x1, waiting for transfers between devices, per_device(): lax.all_to_all(own.reshape(experts, piece, width), 'expert', split_axis=0...  6.99 us
    all_to_all x1, starting transfers between devices, per_device(): lax.all_to_all(own.reshape(experts, piece, width), 'expert', split_axis=0...  6.55 us
    all_to_all x1, starting transfers between devices, per_device(): lax.all_to_all(send_blocks, 'expert', split_axis=1, concat_axis=1, tiled=...  6 us
    all_to_all x1, starting transfers between devices, per_device(): lax.all_to_all(send_weights, 'expert', split_axis=1, concat_axis=1, tiled...  4.96 us
    dot_general x3, matrix products, one_slot(): corr = jnp.dot(left.T, right, preferred_element_type=jnp.float32)  4.58 us
    another operation x1, loops' own time, energies(): return lax.map(one_slot, (other, part_w))  4.39 us
    all_to_all x1, waiting for transfers between devices, per_device(): lax.all_to_all(send_weights, 'expert', split_axis=1, concat_axis=1, tiled...  2.37 us
  transfers between devices with their start and end apart: 3, of which 3 were waited for; matrix products, arithmetic and copies ran while one was open for 8% of the time, Pallas kernels for 0%

commit v1 on v0

--- a/solution.py
+++ b/solution.py
@@ -1,7 +1,132 @@
+import functools
+
 import jax
 import jax.numpy as jnp
 from jax import lax
+from jax.experimental import pallas as pl
+from jax.experimental.pallas import tpu as pltpu
 from jax.sharding import PartitionSpec as P
+
+F32 = jnp.float32
+BF16 = jnp.bfloat16
+CHUNK = 256
+
+
+def gram_kernel(
+    experts, x_ref, routing_ref, pairs_ref, out_ref,
+    z_ref, wt_ref, send_ref, recv_ref, mean_ref, rate_ref, send_sem, recv_sem,
+):
+    me = lax.axis_index("expert")
+    tokens, width = x_ref.shape
+    slots = wt_ref.shape[0]
+
+    barrier = pltpu.get_barrier_semaphore()
+    for s in range(1, experts):
+        pl.semaphore_signal(
+            barrier, inc=1, device_id={"expert": lax.rem(me + s, experts)},
+            device_id_type=pl.DeviceIdType.MESH,
+        )
+
+    lane = lax.broadcasted_iota(jnp.int32, (tokens, 128), 1)
+    label = lax.rem(lane + me, experts)
+    hit = jnp.zeros((tokens, 128), jnp.bool_)
+    mine = jnp.zeros((tokens, 1), jnp.bool_)
+    for k in range(routing_ref.shape[1]):
+        chosen = routing_ref[:, k:k + 1]
+        hit = hit | (chosen == label)
+        mine = mine | (chosen == me)
+    g = jnp.where(hit, 2.0, 0.5)
+    g_me = jnp.where(mine, 2.0, 0.5)
+    w = jnp.where(lane == 0, 1.0, g * g_me)
+    wt = w.T[:slots, :]
+    wt_ref[...] = wt
+    total = jnp.sum(wt, axis=1, keepdims=True)
+    wt16 = wt.astype(BF16)
+
+    for c in range(0, width, CHUNK):
+        cols = slice(c, c + CHUNK)
+        x = x_ref[:, cols]
+        mean = jnp.dot(wt16, x, preferred_element_type=F32) / total
+        center = mean[0:1, :]
+        y = x.astype(F32) - center
+        sq = y * y
+        high = sq.astype(BF16)
+        low = (sq - high.astype(F32)).astype(BF16)
+        second = (
+            jnp.dot(wt16, high, preferred_element_type=F32)
+            + jnp.dot(wt16, low, preferred_element_type=F32)
+        ) / total
+        moved = mean - center
+        var = jnp.maximum(second - moved * moved, 0.0)
+        mean_ref[:, cols] = mean
+        rate_ref[:, cols] = 1.0 / (jnp.sqrt(var + 1e-06) * jnp.sqrt(total))
+
+    pl.semaphore_wait(barrier, experts - 1)
+
+    copies = []
+    for s in range(1, experts):
+        gram = jnp.zeros((tokens, tokens), F32)
+        for c in range(0, width, CHUNK):
+            cols = slice(c, c + CHUNK)
+            z = ((x_ref[:, cols].astype(F32) - mean_ref[s:s + 1, cols]) * rate_ref[s:s + 1, cols]).astype(BF16)
+            z_ref[s, :, cols] = z
+            gram += lax.dot_general(z, z, (((1,), (1,)), ((), ())), preferred_element_type=F32)
+        send_ref[s] = (gram * w[:, s:s + 1] * wt_ref[s:s + 1, :]).astype(BF16)
+        copy = pltpu.make_async_remote_copy(
+            src_ref=send_ref.at[s],
+            dst_ref=recv_ref.at[s],
+            send_sem=send_sem.at[s],
+            recv_sem=recv_sem.at[s],
+            device_id={"expert": lax.rem(me + s, experts)},
+            device_id_type=pl.DeviceIdType.MESH,
+        )
+        copy.start()
+        copies.append(copy)
+    for copy in copies:
+        copy.wait()
+
+    for p in range(pairs_ref.shape[1]):
+        partner = pairs_ref[me, p]
+        used = partner >= 0
+        other = jnp.where(used, partner, lax.rem(me + 1, experts))
+        ahead = lax.rem(other - me + experts, experts)
+        behind = lax.rem(me - other + experts, experts)
+        gram = recv_ref[behind]
+        keep = jnp.where(used, 1.0, 0.0).astype(F32)
+        for c in range(0, width, CHUNK):
+            cols = slice(c, c + CHUNK)
+            z = z_ref[ahead, :, cols]
+            product = jnp.dot(gram, z, preferred_element_type=F32)
+            out_ref[p:p + 1, cols] = jnp.sum(product * z.astype(F32), axis=0, keepdims=True) * keep
+
+
+def gram_device(activations, routing, pairs):
+    experts = lax.axis_size("expert")
+    own = activations[0]
+    tokens, width = own.shape
+    count = pairs.shape[1]
+    slots = -(-experts // 8) * 8
+    vmem = pl.BlockSpec(memory_space=pltpu.VMEM)
+    result = pl.pallas_call(
+        functools.partial(gram_kernel, experts),
+        out_shape=jax.ShapeDtypeStruct((count, width), F32),
+        in_specs=[vmem, vmem, pl.BlockSpec(memory_space=pltpu.SMEM)],
+        out_specs=vmem,
+        scratch_shapes=[
+            pltpu.VMEM((experts, tokens, width), BF16),
+            pltpu.VMEM((slots, tokens), F32),
+            pltpu.VMEM((experts, tokens, tokens), BF16),
+            pltpu.VMEM((experts, tokens, tokens), BF16),
+            pltpu.VMEM((slots, width), F32),
+            pltpu.VMEM((slots, width), F32),
+            pltpu.SemaphoreType.DMA((experts,)),
+            pltpu.SemaphoreType.DMA((experts,)),
+        ],
+        compiler_params=pltpu.CompilerParams(
+            collective_id=0, has_side_effects=True, vmem_limit_bytes=32 * 1024 * 1024
+        ),
+    )(own, routing, pairs)
+    return result[None]
 
 
 def weights_for(routing, experts):
@@ -38,7 +163,7 @@
     return lax.map(one_slot, (other, part_w))
 
 
-def per_device(activations, routing, pairs):
+def slice_device(activations, routing, pairs):
     own = activations[0]
     experts = lax.axis_size("expert")
     me = lax.axis_index("expert")
@@ -64,6 +189,16 @@
     return result[None]
 
 
+def per_device(activations, routing, pairs):
+    experts = lax.axis_size("expert")
+    tokens, width = activations.shape[1:]
+    gram_sends = experts * tokens * tokens
+    slice_sends = (1 + pairs.shape[1]) * tokens * width
+    if gram_sends < slice_sends:
+        return gram_device(activations, routing, pairs)
+    return slice_device(activations, routing, pairs)
+
+
 def solution(mesh):
     return jax.shard_map(
         per_device,

time: 74.6 us -> 21.8 us (0.29)
  waiting for transfers between devices: 37 us -> 0 us
  Pallas kernels: 0 us -> 19.1 us
  starting transfers between devices: 17.5 us -> 0 us
  other arithmetic: 5.44 us -> 0 us
  matrix products: 4.58 us -> 0 us
  loops' own time: 4.39 us -> 0 us
  local copies, waits for them, and re-layouts: 5.17 us -> 2.5 us
    all_to_all x3 -> x0, waiting for transfers between devices: 37 us -> none  [the longest x1 27.6 us: per_device(): lax.all_to_all(send_blocks, 'expert', split_axis=1, concat_axis=1, tiled=...]
    pallas_call x0 -> x1, Pallas kernels: none -> 19.1 us  [gram_device(): pl.pallas_call(functools.partial(gram_kernel, experts), out_shape=jax.Sha...]
    all_to_all x3 -> x0, starting transfers between devices: 17.5 us -> none  [the longest x1 6.55 us: per_device(): lax.all_to_all(own.reshape(experts, piece, width), 'expert', split_axis=0...]
    dot_general x3 -> x0, matrix products: 4.58 us -> none  [one_slot(): corr = jnp.dot(left.T, right, preferred_element_type=jnp.float32)]
    another operation x1 -> x0, loops' own time: 4.39 us -> none  [energies(): return lax.map(one_slot, (other, part_w))]
    reduce_sum x12 -> x0, other arithmetic: 3.83 us -> none  [the longest x3 2.06 us: one_slot(): total = jnp.sum(weights)]
    gather x4 -> x0, local copies, waits for them, and re-layouts: 2.38 us -> none  [the longest x2 1.73 us: per_device(): send_blocks = columns[safe]]
    unnamed x4 -> x6, local copies, waits for them, and re-layouts: 0.01 us -> 1.88 us
  transfers between devices with their start and end apart: 3 -> 0, of which waited for: 3 -> 0; matrix products, arithmetic and copies ran while one was open for 8% -> 0% of each run, Pallas kernels for 0% -> 0%
where the time goes in v1:
time: 21.8 us; the launch traced here: 21.6 us
  Pallas kernels  19.1 us (88%)
  local copies, waits for them, and re-layouts  2.5 us (11%)
    pallas_call x1, Pallas kernels, gram_device(): pl.pallas_call(functools.partial(gram_kernel, experts), out_shape=jax.Sha...  19.1 us
    unnamed x6, local copies, waits for them, and re-layouts  1.88 us
    broadcast_in_dim x1, local copies, waits for them, and re-layouts, gram_device(): return result[None]  0.63 us

profile of v1, /device:TPU:13, one launch (start us, length us, event | category | flops | bytes accessed | tf_op | source)
XLA Modules:
  0.0 21.6 jit_solution(10624283515949335536)
XLA Ops:
  0.0 0.0 copy-start.1
  0.0 0.8 %copy.5.pairs_ref = s32[16,3]{1,0:T(8,128)S(1)} copy(s32[16,3]{0,1:T(4,128)} %param.5) | data formatting | bytes 384 | tf_op args[2]
  0.8 0.0 copy-done.1
  0.8 0.1 copy.4.routing_ref
  0.9 0.0 copy-start
  0.9 1.0 %copy-done = bf16[1,128,1536]{2,1,0:T(8,128)(2,1)S(1)} copy-done((bf16[1,128,1536]{2,1,0:T(8,128)(2,1)S(1)}, bf16[1,128,1536]{2,1,0:T(8,128)(2,1)}, u32[]{:S(2)}) %copy-start) | copy-done | bytes 393240
  1.9 19.1 %shard_map.37 = f32[3,1536]{1,0:T(4,128)S(1)} custom-call(bf16[128,1536]{1,0:T(8,128)(2,1)S(1)} %bitcast.2, s32[128,6]{1,0:T(8,128)S(1)} %copy.4.routing_ref, s32[16,3]{1,0:T(8,128)S(1)} %copy.5.pairs_ref), custom_call_target="tpu_custom_call" | custom-call | tf_op jit(solution)/shard_map/pallas_call | solution.py:110
  21.0 0.6 %copy.6 = f32[1,3,1536]{2,0,1:T(1,128)} copy(f32[1,3,1536]{2,1,0:T(4,128)S(1)} %bitcast.3) | data formatting | bytes 36864 | tf_op jit(solution)/shard_map/broadcast_in_dim | solution.py:129
Async XLA Ops:
  0.0 0.8 %copy-start.1 = (s32[128,6]{0,1:T(8,128)S(1)}, s32[128,6]{0,1:T(8,128)}, u32[]{:S(2)}) copy-start(s32[128,6]{0,1:T(8,128)} %param.4) | copy-start | bytes 9220
  0.9 1.0 %copy-start = (bf16[1,128,1536]{2,1,0:T(8,128)(2,1)S(1)}, bf16[1,128,1536]{2,1,0:T(8,128)(2,1)}, u32[]{:S(2)}) copy-start(bf16[1,128,1536]{2,1,0:T(8,128)(2,1)} %param.3) | copy-start | bytes 1179652

commit v2 on v1

--- a/solution.py
+++ b/solution.py
@@ -10,39 +10,59 @@
 F32 = jnp.float32
 BF16 = jnp.bfloat16
 CHUNK = 256
+AHEAD = 4
 
 
 def gram_kernel(
-    experts, x_ref, routing_ref, pairs_ref, out_ref,
-    z_ref, wt_ref, send_ref, recv_ref, mean_ref, rate_ref, send_sem, recv_sem,
+    experts, order, x_hbm, routing_ref, pairs_ref, out_ref,
+    x_ref, z_ref, wt_ref, send_ref, recv_ref, edge_ref, edge_in_ref, mean_ref, rate_ref,
+    load_sem, send_sem, recv_sem, edge_sem, edge_in_sem,
 ):
     me = lax.axis_index("expert")
     tokens, width = x_ref.shape
     slots = wt_ref.shape[0]
+    load = pltpu.make_async_copy(x_hbm, x_ref, load_sem.at[0])
+    load.start()
+    half = experts // 2 if experts % 2 == 0 else experts
+
+    def split(index):
+        upper = jnp.where(index >= half, 1, 0)
+        return upper, index - upper * half
+
+    def wrap(value, count):
+        return jnp.where(value >= count, value - count, value)
+
+    my_upper, my_place = split(me)
+
+    def toward(s):
+        upper, place = (s // half, s % half) if isinstance(s, int) else split(s)
+        return wrap(my_upper + upper, 2) * half + wrap(my_place + place, half)
+
+    def between(start, end):
+        return wrap(end[0] - start[0] + 2, 2) * half + wrap(end[1] - start[1] + half, half)
 
     barrier = pltpu.get_barrier_semaphore()
     for s in range(1, experts):
         pl.semaphore_signal(
-            barrier, inc=1, device_id={"expert": lax.rem(me + s, experts)},
+            barrier, inc=1, device_id={"expert": toward(s)},
             device_id_type=pl.DeviceIdType.MESH,
         )
 
-    lane = lax.broadcasted_iota(jnp.int32, (tokens, 128), 1)
-    label = lax.rem(lane + me, experts)
-    hit = jnp.zeros((tokens, 128), jnp.bool_)
-    mine = jnp.zeros((tokens, 1), jnp.bool_)
-    for k in range(routing_ref.shape[1]):
-        chosen = routing_ref[:, k:k + 1]
+    slot = lax.broadcasted_iota(jnp.int32, (slots, tokens), 0)
+    label = toward(slot)
+    hit = jnp.zeros((slots, tokens), jnp.bool_)
+    mine = jnp.zeros((1, tokens), jnp.bool_)
+    for k in range(routing_ref.shape[0]):
+        chosen = routing_ref[k:k + 1, :]
         hit = hit | (chosen == label)
         mine = mine | (chosen == me)
-    g = jnp.where(hit, 2.0, 0.5)
-    g_me = jnp.where(mine, 2.0, 0.5)
-    w = jnp.where(lane == 0, 1.0, g * g_me)
-    wt = w.T[:slots, :]
+    wt = jnp.where(slot == 0, 1.0, jnp.where(hit, 2.0, 0.5) * jnp.where(mine, 2.0, 0.5))
     wt_ref[...] = wt
+    w = wt.T
     total = jnp.sum(wt, axis=1, keepdims=True)
     wt16 = wt.astype(BF16)
 
+    load.wait()
     for c in range(0, width, CHUNK):
         cols = slice(c, c + CHUNK)
         x = x_ref[:, cols]
@@ -61,43 +81,72 @@
         mean_ref[:, cols] = mean
         rate_ref[:, cols] = 1.0 / (jnp.sqrt(var + 1e-06) * jnp.sqrt(total))
 
-    pl.semaphore_wait(barrier, experts - 1)
+    mid = tokens // 2
+    row = lax.broadcasted_iota(jnp.int32, (mid, tokens), 0)
+    col = lax.broadcasted_iota(jnp.int32, (mid, tokens), 1)
+    factor = jnp.where(row == col, 1.0, 2.0)
 
     copies = []
-    for s in range(1, experts):
-        gram = jnp.zeros((tokens, tokens), F32)
+
+    def send(s):
+        for source, target, out_sem, in_sem in (
+            (send_ref, recv_ref, send_sem, recv_sem), (edge_ref, edge_in_ref, edge_sem, edge_in_sem)
+        ):
+            copy = pltpu.make_async_remote_copy(
+                src_ref=source.at[s],
+                dst_ref=target.at[s],
+                send_sem=out_sem.at[s],
+                recv_sem=in_sem.at[s],
+                device_id={"expert": toward(s)},
+                device_id_type=pl.DeviceIdType.MESH,
+            )
+            copy.start()
+            copies.append(copy)
+
+    for n, s in enumerate(order):
         for c in range(0, width, CHUNK):
             cols = slice(c, c + CHUNK)
-            z = ((x_ref[:, cols].astype(F32) - mean_ref[s:s + 1, cols]) * rate_ref[s:s + 1, cols]).astype(BF16)
-            z_ref[s, :, cols] = z
-            gram += lax.dot_general(z, z, (((1,), (1,)), ((), ())), preferred_element_type=F32)
-        send_ref[s] = (gram * w[:, s:s + 1] * wt_ref[s:s + 1, :]).astype(BF16)
-        copy = pltpu.make_async_remote_copy(
-            src_ref=send_ref.at[s],
-            dst_ref=recv_ref.at[s],
-            send_sem=send_sem.at[s],
-            recv_sem=recv_sem.at[s],
-            device_id={"expert": lax.rem(me + s, experts)},
-            device_id_type=pl.DeviceIdType.MESH,
-        )
-        copy.start()
-        copies.append(copy)
+            z_ref[s, :, cols] = (
+                (x_ref[:, cols].astype(F32) - mean_ref[s:s + 1, cols]) * rate_ref[s:s + 1, cols]
+            ).astype(BF16)
+        z = z_ref[s]
+        gram = lax.dot_general(z, z, (((1,), (1,)), ((), ())), preferred_element_type=F32)
+        gram = gram * w[:, s:s + 1] * wt_ref[s:s + 1, :]
+        top = gram[:mid, :] * factor
+        below = pltpu.roll(gram[mid:, :], mid, 1)
+        send_ref[s] = jnp.where(row <= col, top, below * 2.0).astype(BF16)
+        edge_ref[s] = jnp.sum(jnp.where(row == col, below, 0.0), axis=0, keepdims=True)
+        if n + 1 == AHEAD:
+            pl.semaphore_wait(barrier, experts - 1)
+            for earlier in order[:n]:
+                send(earlier)
+        if n + 1 >= AHEAD:
+            send(s)
     for copy in copies:
         copy.wait()
 
-    for p in range(pairs_ref.shape[1]):
-        partner = pairs_ref[me, p]
+    for p in range(pairs_ref.shape[0]):
+        partner = pairs_ref[p, me]
         used = partner >= 0
-        other = jnp.where(used, partner, lax.rem(me + 1, experts))
-        ahead = lax.rem(other - me + experts, experts)
-        behind = lax.rem(me - other + experts, experts)
-        gram = recv_ref[behind]
+        other = jnp.where(used, partner, toward(1))
+        ahead = between((my_upper, my_place), split(other))
+        behind = between(split(other), (my_upper, my_place))
+        packed = recv_ref[behind].astype(F32)
+        edge = jnp.where(row == col, edge_in_ref[behind], 0.0)
+        lower = pltpu.roll(jnp.where(row > col, packed, edge), mid, 1)
+        gram = jnp.concatenate([jnp.where(row <= col, packed, 0.0), lower], axis=0).astype(BF16)
         keep = jnp.where(used, 1.0, 0.0).astype(F32)
         for c in range(0, width, CHUNK):
             cols = slice(c, c + CHUNK)
             z = z_ref[ahead, :, cols]
             product = jnp.dot(gram, z, preferred_element_type=F32)
-            out_ref[p:p + 1, cols] = jnp.sum(product * z.astype(F32), axis=0, keepdims=True) * keep
+            out_ref[p, :, cols] = jnp.sum(product * z.astype(F32), axis=0, keepdims=True) * keep
+
+
+def sending_order(experts):
+    half = experts // 2
+    far, near = list(range(half, experts)), list(range(1, half))
+    return [s for pair in zip(far, near) for s in pair] + far[len(near):]
 
 
 def gram_device(activations, routing, pairs):
@@ -106,27 +155,34 @@
     tokens, width = own.shape
     count = pairs.shape[1]
     slots = -(-experts // 8) * 8
+    order = sending_order(experts)
     vmem = pl.BlockSpec(memory_space=pltpu.VMEM)
     result = pl.pallas_call(
-        functools.partial(gram_kernel, experts),
-        out_shape=jax.ShapeDtypeStruct((count, width), F32),
-        in_specs=[vmem, vmem, pl.BlockSpec(memory_space=pltpu.SMEM)],
+        functools.partial(gram_kernel, experts, order),
+        out_shape=jax.ShapeDtypeStruct((count, 1, width), F32),
+        in_specs=[pl.BlockSpec(memory_space=pltpu.HBM), vmem, pl.BlockSpec(memory_space=pltpu.SMEM)],
         out_specs=vmem,
         scratch_shapes=[
+            pltpu.VMEM((tokens, width), BF16),
             pltpu.VMEM((experts, tokens, width), BF16),
             pltpu.VMEM((slots, tokens), F32),
-            pltpu.VMEM((experts, tokens, tokens), BF16),
-            pltpu.VMEM((experts, tokens, tokens), BF16),
+            pltpu.VMEM((experts, tokens // 2, tokens), BF16),
+            pltpu.VMEM((experts, tokens // 2, tokens), BF16),
+            pltpu.VMEM((experts, 1, tokens), F32),
+            pltpu.VMEM((experts, 1, tokens), F32),
             pltpu.VMEM((slots, width), F32),
             pltpu.VMEM((slots, width), F32),
+            pltpu.SemaphoreType.DMA((width // CHUNK,)),
+            pltpu.SemaphoreType.DMA((experts,)),
+            pltpu.SemaphoreType.DMA((experts,)),
             pltpu.SemaphoreType.DMA((experts,)),
             pltpu.SemaphoreType.DMA((experts,)),
         ],
         compiler_params=pltpu.CompilerParams(
-            collective_id=0, has_side_effects=True, vmem_limit_bytes=32 * 1024 * 1024
+            collective_id=0, has_side_effects=True, vmem_limit_bytes=60 * 1024 * 1024
         ),
-    )(own, routing, pairs)
-    return result[None]
+    )(own, routing.T, pairs.T)
+    return result.reshape(1, count, width)
 
 
 def weights_for(routing, experts):

time: 21.8 us -> 18.1 us (0.83)
  the two profiles are of different devices: /device:TPU:13 before, /device:TPU:1 now
where the time goes in v2:
time: 18.1 us; the launch traced here: 17.8 us
  Pallas kernels  16.5 us (91%)
  local copies, waits for them, and re-layouts  1.33 us (7%)
    pallas_call x1, Pallas kernels, gram_device(): pl.pallas_call(functools.partial(gram_kernel, experts, order), out_shape=...  16.5 us
    unnamed x1, local copies, waits for them, and re-layouts  1.33 us

profile of v2, /device:TPU:1, one launch (start us, length us, event | category | flops | bytes accessed | tf_op | source)
XLA Modules:
  0.0 17.8 jit_solution(987315626269192279)
XLA Ops:
  0.0 16.5 %shard_map.37 = f32[3,1,1536]{2,1,0:T(1,128)} custom-call(bf16[128,1536]{1,0:T(8,128)(2,1)} %bitcast.4, s32[6,128]{1,0:T(8,128)} %bitcast.6, s32[3,16]{1,0:T(4,128)} %bitcast.7), custom_call_target="tpu_custom_call" | custom-call | tf_op jit(solution)/shard_map/pallas_call | solution.py:160
  16.5 1.3 %copy.5 = f32[1,3,1536]{2,0,1:T(1,128)} copy(f32[1,3,1536]{2,0,1:T(1,128)} %bitcast.5) | data formatting | bytes 36864

commit v3 on v2

--- a/solution.py
+++ b/solution.py
@@ -21,7 +21,7 @@
     me = lax.axis_index("expert")
     tokens, width = x_ref.shape
     slots = wt_ref.shape[0]
-    load = pltpu.make_async_copy(x_hbm, x_ref, load_sem.at[0])
+    load = pltpu.make_async_copy(x_hbm, x_ref, load_sem)
     load.start()
     half = experts // 2 if experts % 2 == 0 else experts
 
@@ -60,48 +60,50 @@
     wt_ref[...] = wt
     w = wt.T
     total = jnp.sum(wt, axis=1, keepdims=True)
+    inverse = 1.0 / total
+    root = jnp.sqrt(inverse)
     wt16 = wt.astype(BF16)
+    wt_twice = jnp.concatenate([wt16, wt16], axis=1)
 
     load.wait()
     for c in range(0, width, CHUNK):
         cols = slice(c, c + CHUNK)
         x = x_ref[:, cols]
-        mean = jnp.dot(wt16, x, preferred_element_type=F32) / total
+        mean = jnp.dot(wt16, x, preferred_element_type=F32) * inverse
         center = mean[0:1, :]
         y = x.astype(F32) - center
         sq = y * y
         high = sq.astype(BF16)
         low = (sq - high.astype(F32)).astype(BF16)
         second = (
-            jnp.dot(wt16, high, preferred_element_type=F32)
-            + jnp.dot(wt16, low, preferred_element_type=F32)
-        ) / total
+            jnp.dot(wt_twice, jnp.concatenate([high, low], axis=0), preferred_element_type=F32)
+        ) * inverse
         moved = mean - center
         var = jnp.maximum(second - moved * moved, 0.0)
         mean_ref[:, cols] = mean
-        rate_ref[:, cols] = 1.0 / (jnp.sqrt(var + 1e-06) * jnp.sqrt(total))
+        rate_ref[:, cols] = lax.rsqrt(var + 1e-06) * root
 
     mid = tokens // 2
     row = lax.broadcasted_iota(jnp.int32, (mid, tokens), 0)
     col = lax.broadcasted_iota(jnp.int32, (mid, tokens), 1)
     factor = jnp.where(row == col, 1.0, 2.0)
 
-    copies = []
+    arrays = (
+        (send_ref, recv_ref, send_sem, recv_sem),
+        (edge_ref, edge_in_ref, edge_sem, edge_in_sem),
+    )
 
     def send(s):
-        for source, target, out_sem, in_sem in (
-            (send_ref, recv_ref, send_sem, recv_sem), (edge_ref, edge_in_ref, edge_sem, edge_in_sem)
-        ):
+        for source, target, out_sem, in_sem in arrays:
             copy = pltpu.make_async_remote_copy(
                 src_ref=source.at[s],
                 dst_ref=target.at[s],
-                send_sem=out_sem.at[s],
-                recv_sem=in_sem.at[s],
+                send_sem=out_sem,
+                recv_sem=in_sem,
                 device_id={"expert": toward(s)},
                 device_id_type=pl.DeviceIdType.MESH,
             )
             copy.start()
-            copies.append(copy)
 
     for n, s in enumerate(order):
         for c in range(0, width, CHUNK):
@@ -122,8 +124,21 @@
                 send(earlier)
         if n + 1 >= AHEAD:
             send(s)
-    for copy in copies:
-        copy.wait()
+
+    others = pl.ds(1, experts - 1)
+    exchanges = [
+        pltpu.make_async_remote_copy(
+            src_ref=source.at[others],
+            dst_ref=target.at[others],
+            send_sem=out_sem,
+            recv_sem=in_sem,
+            device_id={"expert": toward(1)},
+            device_id_type=pl.DeviceIdType.MESH,
+        )
+        for source, target, out_sem, in_sem in arrays
+    ]
+    for exchange in exchanges:
+        exchange.wait_recv()
 
     for p in range(pairs_ref.shape[0]):
         partner = pairs_ref[p, me]
@@ -142,11 +157,14 @@
             product = jnp.dot(gram, z, preferred_element_type=F32)
             out_ref[p, :, cols] = jnp.sum(product * z.astype(F32), axis=0, keepdims=True) * keep
 
+    for exchange in exchanges:
+        exchange.wait_send()
+
 
 def sending_order(experts):
     half = experts // 2
     far, near = list(range(half, experts)), list(range(1, half))
-    return [s for pair in zip(far, near) for s in pair] + far[len(near):]
+    return far + near
 
 
 def gram_device(activations, routing, pairs):
@@ -172,11 +190,11 @@
             pltpu.VMEM((experts, 1, tokens), F32),
             pltpu.VMEM((slots, width), F32),
             pltpu.VMEM((slots, width), F32),
-            pltpu.SemaphoreType.DMA((width // CHUNK,)),
-            pltpu.SemaphoreType.DMA((experts,)),
-            pltpu.SemaphoreType.DMA((experts,)),
-            pltpu.SemaphoreType.DMA((experts,)),
-            pltpu.SemaphoreType.DMA((experts,)),
+            pltpu.SemaphoreType.DMA,
+            pltpu.SemaphoreType.DMA,
+            pltpu.SemaphoreType.DMA,
+            pltpu.SemaphoreType.DMA,
+            pltpu.SemaphoreType.DMA,
         ],
         compiler_params=pltpu.CompilerParams(
             collective_id=0, has_side_effects=True, vmem_limit_bytes=60 * 1024 * 1024

time: 18.1 us -> 17.3 us (0.956)
  the two profiles are of different devices: /device:TPU:1 before, /device:TPU:0 now
where the time goes in v3:
time: 17.3 us; the launch traced here: 17.1 us
  Pallas kernels  15.8 us (91%)
  local copies, waits for them, and re-layouts  1.33 us (8%)
    pallas_call x1, Pallas kernels, gram_device(): pl.pallas_call(functools.partial(gram_kernel, experts, order), out_shape=...  15.8 us
    unnamed x1, local copies, waits for them, and re-layouts  1.33 us

profile of v3, /device:TPU:0, one launch (start us, length us, event | category | flops | bytes accessed | tf_op | source)
XLA Modules:
  0.0 17.1 jit_solution(14400718410873173)
XLA Ops:
  0.0 15.8 %shard_map.37 = f32[3,1,1536]{2,1,0:T(1,128)} custom-call(bf16[128,1536]{1,0:T(8,128)(2,1)} %bitcast.4, s32[6,128]{1,0:T(8,128)} %bitcast.6, s32[3,16]{1,0:T(4,128)} %bitcast.7), custom_call_target="tpu_custom_call" | custom-call | tf_op jit(solution)/shard_map/pallas_call | solution.py:178
  15.8 1.3 %copy.5 = f32[1,3,1536]{2,0,1:T(1,128)} copy(f32[1,3,1536]{2,0,1:T(1,128)} %bitcast.5) | data formatting | bytes 36864
